TPU v7x, 32 devices: a whole 2x2x4 slice. The times are simulated.
32 devices in a mesh: rec: 4 (over z), tm: 8 (over y, x, core).
Axes of the slice: x: 2, y: 2, z: 4, core: 2. Of those that a mesh axis runs over, the one named last changes fastest.
Arguments:
- audio: float32 [4, 40960], P('rec', 'tm'), may hold values from -100 to 100, as said below
- conv0_weight: float32 [10, 512], replicated, may hold values from -2 to 2
- norm_gain: float32 [512], replicated, may hold values from 0.25 to 1.75
- norm_bias: float32 [512], replicated, may hold values from -3 to 3
- conv1_weight: bfloat16 [1536, 512], replicated, may hold values from -0.25 to 0.25
- conv2_weight: bfloat16 [1536, 512], replicated, may hold values from -0.25 to 0.25
- cotangent: bfloat16 [4, 2048, 512], P('rec', 'tm'), may hold values from -0.09375 to 0.09375
Outputs:
- features: bfloat16 [4, 2048, 512], P('rec', 'tm')
- grad_conv0: float32 [10, 512], replicated
- grad_gain: float32 [512], replicated
- grad_bias: float32 [512], replicated
- grad_conv1: float32 [1536, 512], replicated
- grad_conv2: float32 [1536, 512], replicated
Inputs may be any that keep to these rules, and one draw needn't show every extreme that they name: `audio`: recorded waveforms, one row a recording.
All inputs are finite; a program needn't handle non-finite values.
Results may differ from a plain program's by a relative error of at most 0.0095.
Values may be sent and summed in bfloat16 or wider, within the bound.
A program may use at most 64 MiB of HBM per device.

v0:
```python
import jax
import jax.numpy as jnp
from jax import lax
from jax.sharding import PartitionSpec as P

EPS = 1e-05
HIGH = lax.Precision.HIGHEST


def from_behind(value, axis, steps):
    count = lax.axis_size(axis)
    leading, last = (max(0, -steps), min(count, count - steps))
    return lax.ppermute(value, axis, [(source, source + steps) for source in range(leading, last)])


def gelu_slope(value):
    return (
        0.5 * (1.0 + lax.erf(value * 0.7071067811865476))
        + value * jnp.exp(-0.5 * value * value) * 0.3989422804014327
    )


def stride_conv(active, weight):
    records, frames_in, channels = active.shape
    edge_row = from_behind(active[:, :1, :], "tm", -1)
    pairs = active.reshape(records, frames_in // 2, 2 * channels)
    following = jnp.concatenate([pairs[:, 1:, :channels], edge_row], 1)
    output = jnp.einsum(
        "rtk,kc->rtc", pairs, weight[: 2 * channels], preferred_element_type=jnp.float32
    )
    output = output + jnp.einsum(
        "rtk,kc->rtc", following, weight[2 * channels :], preferred_element_type=jnp.float32
    )
    return (pairs, following, output)


def weight_grad(pairs, following, delta):
    upper = jnp.einsum("rtk,rtc->kc", pairs, delta, preferred_element_type=jnp.float32)
    lower = jnp.einsum("rtk,rtc->kc", following, delta, preferred_element_type=jnp.float32)
    return jnp.concatenate([upper, lower], 0)


def stride_back(delta, weight):
    records, frames_out, channels = delta.shape
    edge_row = from_behind(delta[:, -1:, :], "tm", 1)
    before = jnp.concatenate([edge_row, delta[:, :-1, :]], 1)
    back_pairs = jnp.einsum(
        "rtc,kc->rtk", delta, weight[: 2 * channels], preferred_element_type=jnp.float32
    )
    shifted = jnp.einsum(
        "rtc,kc->rtk", before, weight[2 * channels :], preferred_element_type=jnp.float32
    )
    even_rows = back_pairs[:, :, :channels] + shifted
    joined = jnp.concatenate([even_rows, back_pairs[:, :, channels:]], 2)
    return joined.reshape(records, 2 * frames_out, channels)


def shards(audio, conv0_weight, norm_gain, norm_bias, conv1_weight, conv2_weight, cotangent):
    records = audio.shape[0]
    blocks = audio.reshape(records, audio.shape[1] // 5, 5)
    count = float(blocks.shape[1] * lax.axis_size("tm"))
    sample_edge = from_behind(blocks[:, :1, :], "tm", -1)
    following = jnp.concatenate([blocks[:, 1:, :], sample_edge], 1)
    patches = jnp.concatenate([blocks, following], 2)
    pre_norm = jnp.einsum("rtk,kc->rtc", patches, conv0_weight, precision=HIGH)
    first, second = lax.psum((jnp.sum(pre_norm, 1), jnp.sum(pre_norm * pre_norm, 1)), "tm")
    mean = first / count
    variance = second / count - mean * mean
    centered = pre_norm - mean[:, None, :]
    inverse = lax.rsqrt(variance + EPS)
    normed = centered * inverse[:, None, :]
    shifted_norm = normed * norm_gain + norm_bias
    act0 = jax.nn.gelu(shifted_norm, approximate=False).astype(jnp.bfloat16)
    pairs1, follow1, pre1 = stride_conv(act0, conv1_weight)
    act1 = jax.nn.gelu(pre1, approximate=False).astype(jnp.bfloat16)
    pairs2, follow2, pre2 = stride_conv(act1, conv2_weight)
    features = jax.nn.gelu(pre2, approximate=False).astype(jnp.bfloat16)
    delta2 = (cotangent.astype(jnp.float32) * gelu_slope(pre2)).astype(jnp.bfloat16)
    grad_two = weight_grad(pairs2, follow2, delta2)
    back1 = stride_back(delta2, conv2_weight)
    delta1 = (back1 * gelu_slope(pre1)).astype(jnp.bfloat16)
    grad_one = weight_grad(pairs1, follow1, delta1)
    back0 = stride_back(delta1, conv1_weight)
    dnorm = back0 * gelu_slope(shifted_norm)
    local_one = jnp.sum(dnorm, 1)
    local_two = jnp.sum(dnorm * normed, 1)
    sum_one, sum_two = lax.psum((local_one, local_two), "tm")
    scale = norm_gain * inverse
    dpre = scale[:, None, :] * (
        dnorm - (sum_one / count)[:, None, :] - normed * (sum_two / count)[:, None, :]
    )
    grad_zero = jnp.einsum("rtk,rtc->kc", patches, dpre, precision=HIGH)
    norm_terms = jnp.stack([jnp.sum(local_two, 0), jnp.sum(local_one, 0)], 0)
    grad_zero, norm_terms, grad_one, grad_two = lax.psum(
        (grad_zero, norm_terms, grad_one, grad_two), ("rec", "tm")
    )
    return (features, grad_zero, norm_terms[0], norm_terms[1], grad_one, grad_two)


def solution(mesh):
    return jax.shard_map(
        shards,
        mesh=mesh,
        in_specs=(P("rec", "tm"), P(), P(), P(), P(), P(), P("rec", "tm", None)),
        out_specs=(P("rec", "tm", None), P(), P(), P(), P(), P()),
        check_vma=False,
    )
```

profile of v0, /device:TPU:0, one launch (start us, length us, event | category | flops | bytes accessed | tf_op | source)
XLA Modules:
  0.0 249.6 jit_solution(3588708600532290643)
XLA Ops:
  7.2 0.5 broadcast.213
  7.7 1.4 reduce.11
  9.2 0.4 reshape.355
  9.6 1.3 collective-permute-start
  11.3 1.3 collective-permute-done
  12.8 1.9 fusion.93
  14.7 15.5 %all-reduce.3 = (f32[1,512]{1,0:T(1,128)S(1)}, f32[1,512]{1,0:T(1,128)S(1)}) all-reduce(f32[1,512]{1,0:T(1,128)S(1)} %bitcast.99, f32[1,512]{1,0:T(1,128)S(1)} %bitcast.98), channel_id=1, replica_groups=mesh['rec'=4,'tm'=8] {'tm'}, use_global_device_ids=true, to_apply=%region_3.0 | all-reduce | flops 1024 | bytes 8192 | tf_op jit(solution)/shard_map/psum | solution.py:66
  30.2 4.9 %fusion.2 = bf16[1024,512]{1,0:T(8,128)(2,1)S(1)} fusion(f32[1024,512]{1,0:T(8,128)S(1)} %get-tuple-element.24, f32[512]{0:T(512)S(1)} %copy-done.8, f32[512]{0:T(512)S(1)} %copy-done.7, f32[512]{0:T(512)S(1)} %bitcast.82, f32[512]{0:T(512)S(1)} %bitcast.86), kind=kLoop, calls=%fused_computation.6 | loop fusion | flops 36175872 | bytes 3153920 | tf_op jit(solution)/shard_map/convert_element_type | solution.py:73
  35.2 5.7 %fusion.106 = bf16[1,1024,512]{2,1,0:T(8,128)(2,1)} fusion(f32[512]{0:T(512)S(1)} %copy-done.8, f32[512]{0:T(512)S(1)} %copy-done.7, f32[512]{0:T(512)S(1)} %bitcast.83, f32[1024,512]{1,0:T(8,128)S(1)} %get-tuple-element.24, f32[512]{0:T(512)S(1)} %bitcast.87), kind=kLoop, calls=%fused_computation.151 | loop fusion | flops 36175872 | bytes 3153920 | tf_op jit(solution)/shard_map/convert_element_type | solution.py:73
  40.8 1.1 reshape.357
  42.0 0.7 slice.87
  42.7 1.3 collective-permute-start.1
  44.0 3.2 %fusion.47 = f32[512,512]{1,0:T(8,128)} fusion(bf16[512,1024]{1,0:T(8,128)(2,1)} %reshape.357, bf16[1536,512]{1,0:T(8,128)(2,1)} %param.11), kind=kOutput, calls=%fused_computation.81 | convolution fusion | flops 536870912 | bytes 3145728 | tf_op jit(solution)/shard_map/rtk,kc->rtc/dot_general | solution.py:28
  47.2 1.1 reshape.358
  48.3 1.2 slice.86
  49.5 4.9 %fusion.24 = (bf16[512,512]{1,0:T(8,128)(2,1)S(1)}, f32[512,512]{1,0:T(8,128)}) fusion(f32[512,512]{1,0:T(8,128)} %fusion.47, bf16[1536,512]{1,0:T(8,128)(2,1)} %param.11, bf16[1,1,512]{2,1,0:T(2,128)(2,1)S(1)} %collective-permute-done.1, bf16[1,511,512]{2,1,0:T(8,128)(2,1)S(1)} %slice.86), kind=kOutput, calls=%fused_computation.49 | convolution fusion | flops 286785536 | bytes 3670016 | tf_op jit(solution)/shard_map/rtk,kc->rtc/dot_general | solution.py:31
  54.7 1.4 collective-permute-start.2
  56.1 2.5 fusion.44
  58.6 1.0 reshape.361
  59.5 1.0 slice.88
  60.6 2.5 fusion.58
  63.1 0.5 fusion.77
  63.5 3.8 %collective-permute-start.3 = (bf16[1,1,512]{2,1,0:T(2,128)(2,1)S(1)}, bf16[1,1,512]{2,1,0:T(2,128)(2,1)S(1)}, u32[]{:S(2)}, u32[]{:S(2)}) collective-permute-start(bf16[1,1,512]{2,1,0:T(2,128)(2,1)S(1)} %slice.91), channel_id=1, source_target_pairs={{0,1},{1,2},{2,3},{3,4},{4,5},{5,6},{6,7},{8,9},{9,10},{10,11},{11... | collective-permute-start | bytes 3080 | tf_op jit(solution)/shard_map/ppermute | solution.py:13
  67.4 0.3 fusion.75
  67.7 2.0 pad_maximum_fusion.1
  69.7 0.5 convolution_bitcast_fusion.2
  70.2 0.3 fusion.21
  70.7 1.2 reshape.365
  71.8 2.1 fusion.30
  73.9 0.7 fusion.97
  74.7 0.3 copy-done.6
  75.0 0.5 fusion.72
  75.4 2.0 pad_maximum_fusion
  77.4 1.0 copy-done.4
  78.4 1.8 fusion.80
  80.3 3.6 %collective-permute-start.4 = (bf16[1,1,512]{2,1,0:T(2,128)(2,1)S(1)}, bf16[1,1,512]{2,1,0:T(2,128)(2,1)S(1)}, u32[]{:S(2)}, u32[]{:S(2)}) collective-permute-start(bf16[1,1,512]{2,1,0:T(2,128)(2,1)S(1)} %slice.95), channel_id=1, source_target_pairs={{0,1},{1,2},{2,3},{3,4},{4,5},{5,6},{6,7},{8,9},{9,10},{10,11},{11... | collective-permute-start | bytes 3080 | tf_op jit(solution)/shard_map/ppermute | solution.py:13
  83.9 2.0 convolution_bitcast_fusion
  86.0 1.6 fusion.20
  87.6 1.5 pad_maximum_fusion.2
  89.0 2.8 %reshape.367 = f32[1024,512]{1,0:T(8,128)} reshape(f32[1,512,1024]{2,1,0:T(8,128)} %pad_maximum_fusion.2) | data formatting | bytes 4194304 | tf_op jit(solution)/shard_map/reshape | solution.py:55
  91.8 3.6 %fusion.92 = (f32[512]{0:T(512)S(1)}, f32[512]{0:T(512)S(1)}, f32[1024,512]{1,0:T(8,128)}) fusion(f32[512]{0:T(512)S(1)} %bitcast.84, f32[1024,512]{1,0:T(8,128)S(1)} %get-tuple-element.24, f32[512]{0:T(512)S(1)} %bitcast.88, f32[1024,512]{1,0:T(8,128)} %reshape.367, f32[512]{0:T(512)S(1)} %copy-done.8, f32[512]{0:T(512)S(1)} %copy-done.7), kind=kLoop, calls=%fused_computation.146 | loop fusion | flops 8387584 | bytes 6303744 | tf_op jit(solution)/shard_map/reduce_sum | solution.py:85
  95.4 12.9 %all-reduce.2 = (f32[1,512]{1,0:T(1,128)S(1)}, f32[1,512]{1,0:T(1,128)S(1)}) all-reduce(f32[1,512]{1,0:T(1,128)S(1)} %bitcast.93, f32[1,512]{1,0:T(1,128)S(1)} %bitcast.91), channel_id=1, replica_groups=mesh['rec'=4,'tm'=8] {'tm'}, use_global_device_ids=true, to_apply=%region_7.0 | all-reduce | flops 1024 | bytes 8192 | tf_op jit(solution)/shard_map/psum | solution.py:87
  108.3 3.1 %fusion.8 = f32[10,512]{1,0:T(8,128)S(1)} fusion(f32[1024,512]{1,0:T(8,128)} %get-tuple-element.20, f32[1024,512]{1,0:T(8,128)S(1)} %get-tuple-element.24, f32[512]{0:T(512)S(1)} %bitcast.96, f32[512]{0:T(512)S(1)} %bitcast.97, f32[512]{0:T(512)S(1)} %bitcast.95, f32[512]{0:T(512)S(1)} %bitcast.85, f32[512]{0:T(512)S(1)} %bitcast.89, ...), kind=kOutput, calls=%fused_computation.13 | convolution fusion | flops 66060288 | bytes 4265984 | tf_op jit(solution)/shard_map/rtk,rtc->kc/dot_general | solution.py:92
  111.5 42.1 %all-reduce = (f32[10,512]{1,0:T(8,128)}, f32[2,512]{1,0:T(2,128)S(1)}) all-reduce(f32[10,512]{1,0:T(8,128)S(1)} %fusion.8, f32[2,512]{1,0:T(2,128)S(1)} %pad_maximum_fusion.4), channel_id=1, replica_groups=mesh['rec'=4,'tm'=8] {'rec','tm'}, use_global_device_ids=true, to_apply=%region_8.0 | all-reduce | flops 6144 | bytes 49152 | tf_op jit(solution)/shard_map/psum | solution.py:94
  153.6 0.6 fusion.96
  154.2 82.8 %all-reduce.6.cloned.1.call-done = (f32[1536,512]{1,0:T(8,128)}, f32[1536,512]{1,0:T(8,128)}) async-done(((f32[1536,512]{1,0:T(8,128)}, f32[1536,512]{1,0:T(8,128)}), (f32[1536,512]{1,0:T(8,128)}, f32[1536,512]{1,0:T(8,128)})) %all-reduce.6.cloned.1.call-update) | async-done | bytes 6291472 | tf_op jit(solution)/shard_map/psum | solution.py:94
  237.0 4.0 %copy.33 = f32[1536,512]{1,0:T(8,128)} copy(f32[1536,512]{1,0:T(8,128)} %get-tuple-element.35) | data formatting | bytes 6291456
  241.1 1.7 copy.34
  (40 shorter events, 1.1 us)
Async XLA Ops:
  7.2 5.6 %copy-start = (f32[10,512]{1,0:T(8,128)S(1)}, f32[10,512]{1,0:T(8,128)}, u32[]{:S(2)}) copy-start(f32[10,512]{1,0:T(8,128)} %param.8) | copy-start | bytes 61444
  7.2 229.8 %all-reduce.6.cloned.1.call-start = ((), (), s32[]{:S(2)}) async-start(), calls=%async_computation | async-start | bytes 12582912 | tf_op jit(solution)/shard_map/psum | solution.py:94
  9.5 20.7 %copy-start.7 = (f32[512]{0:T(512)S(1)}, f32[512]{0:T(512)}, u32[]{:S(2)}) copy-start(f32[512]{0:T(512)} %param.9) | copy-start | bytes 6148
  9.5 20.7 %copy-start.8 = (f32[512]{0:T(512)S(1)}, f32[512]{0:T(512)}, u32[]{:S(2)}) copy-start(f32[512]{0:T(512)} %param.10) | copy-start | bytes 6148
  9.6 3.0 %collective-permute-start = (f32[1,1,5]{2,1,0:T(1,128)S(1)}, f32[1,1,5]{2,1,0:T(1,128)S(1)}, u32[]{:S(2)}, u32[]{:S(2)}) collective-permute-start(f32[1,1,5]{2,1,0:T(1,128)S(1)} %slice.85), channel_id=1, source_target_pairs={{1,0},{2,1},{3,2},{4,3},{5,4},{6,5},{7,6},{9,8},{10,9},{11,10},{12... | collective-permute-start | bytes 68 | tf_op jit(solution)/shard_map/ppermute | solution.py:13
  42.7 6.8 %collective-permute-start.1 = (bf16[1,1,512]{2,1,0:T(2,128)(2,1)S(1)}, bf16[1,1,512]{2,1,0:T(2,128)(2,1)S(1)}, u32[]{:S(2)}, u32[]{:S(2)}) collective-permute-start(bf16[1,1,512]{2,1,0:T(2,128)(2,1)S(1)} %slice.87), channel_id=1, source_target_pairs={{1,0},{2,1},{3,2},{4,3},{5,4},{6,5},{7,6},{9,8},{10,9},{11,10},{12... | collective-permute-start | bytes 3080 | tf_op jit(solution)/shard_map/ppermute | solution.py:13
  49.5 5.0 %copy-start.5 = (bf16[1,511,512]{2,1,0:T(8,128)(2,1)}, bf16[1,511,512]{2,1,0:T(8,128)(2,1)S(1)}, u32[]{:S(2)}) copy-start(bf16[1,511,512]{2,1,0:T(8,128)(2,1)S(1)} %slice.86) | copy-start | bytes 1569796
  54.6 5.9 %copy-start.9 = (bf16[1,256,512]{2,1,0:T(8,128)(2,1)S(1)}, bf16[1,256,512]{2,1,0:T(8,128)(2,1)}, u32[]{:S(2)}) copy-start(bf16[1,256,512]{2,1,0:T(8,128)(2,1)} %param.13) | copy-start | bytes 786436
  54.7 5.9 %collective-permute-start.2 = (bf16[1,1,512]{2,1,0:T(2,128)(2,1)S(1)}, bf16[1,1,512]{2,1,0:T(2,128)(2,1)S(1)}, u32[]{:S(2)}, u32[]{:S(2)}) collective-permute-start(bf16[1,1,512]{2,1,0:T(2,128)(2,1)S(1)} %slice.89), channel_id=1, source_target_pairs={{1,0},{2,1},{3,2},{4,3},{5,4},{6,5},{7,6},{9,8},{10,9},{11,10},{12... | collective-permute-start | bytes 3080 | tf_op jit(solution)/shard_map/ppermute | solution.py:13
  63.5 6.7 %collective-permute-start.3 = (bf16[1,1,512]{2,1,0:T(2,128)(2,1)S(1)}, bf16[1,1,512]{2,1,0:T(2,128)(2,1)S(1)}, u32[]{:S(2)}, u32[]{:S(2)}) collective-permute-start(bf16[1,1,512]{2,1,0:T(2,128)(2,1)S(1)} %slice.91), channel_id=1, source_target_pairs={{0,1},{1,2},{2,3},{3,4},{4,5},{5,6},{6,7},{8,9},{9,10},{10,11},{11... | collective-permute-start | bytes 3080 | tf_op jit(solution)/shard_map/ppermute | solution.py:13
  67.7 2.0 copy-start.3
  71.8 2.1 copy-start.1
  73.9 1.0 copy-start.6
  77.4 1.0 copy-start.4
  80.3 5.7 %collective-permute-start.4 = (bf16[1,1,512]{2,1,0:T(2,128)(2,1)S(1)}, bf16[1,1,512]{2,1,0:T(2,128)(2,1)S(1)}, u32[]{:S(2)}, u32[]{:S(2)}) collective-permute-start(bf16[1,1,512]{2,1,0:T(2,128)(2,1)S(1)} %slice.95), channel_id=1, source_target_pairs={{0,1},{1,2},{2,3},{3,4},{4,5},{5,6},{6,7},{8,9},{9,10},{10,11},{11... | collective-permute-start | bytes 3080 | tf_op jit(solution)/shard_map/ppermute | solution.py:13
  237.0 4.0 %copy-start.2 = (f32[1536,512]{1,0:T(8,128)S(1)}, f32[1536,512]{1,0:T(8,128)}, u32[]{:S(2)}) copy-start(f32[1536,512]{1,0:T(8,128)} %get-tuple-element.36) | copy-start | bytes 9437188
Sparse Core Ops, SparseCore 0:
  77.5 159.4 all-reduce.5
where the time goes:
time: 251 us; the launch traced here: 250 us
  waiting for transfers between devices  84.2 us (34%)
  blocking collectives  70.5 us (28%)
  other arithmetic  25.2 us (10%)
  matrix products  24.5 us (10%)
  local copies, waits for them, and re-layouts  19.4 us (8%)
  between operations  14.3 us (6%)
  starting transfers between devices  11.5 us (5%)
    psum x1, waiting for transfers between devices, shards(): lax.psum((grad_zero, norm_terms, grad_one, grad_two), ('rec', 'tm'))  82.8 us
    psum x1, blocking collectives, shards(): lax.psum((grad_zero, norm_terms, grad_one, grad_two), ('rec', 'tm'))  42.1 us
    psum x1, blocking collectives, shards(): lax.psum((jnp.sum(pre_norm, 1), jnp.sum(pre_norm * pre_norm, 1)), 'tm')  15.5 us
    psum x1, blocking collectives, shards(): sum_one, sum_two = lax.psum((local_one, local_two), 'tm')  12.9 us
    ppermute x5, starting transfers between devices, from_behind(): lax.ppermute(value, axis, [(source, source + steps) for source in range(l...  11.5 us
    convert_element_type x2, other arithmetic, shards(): act0 = jax.nn.gelu(shifted_norm, approximate=False).astype(jnp.bfloat16)  10.6 us
    unnamed x23, local copies, waits for them, and re-layouts  7.54 us
    dot_general x2, matrix products, stride_conv(): jnp.einsum('rtk,kc->rtc', following, weight[2 * channels:], preferred_ele...  7.41 us
  transfers between devices with their start and end apart: 6, of which 2 were waited for; matrix products, arithmetic and copies ran while one was open for 12% of the time, Pallas kernels for 0%

commit v1 on v0

v1 whole, which is shorter than its diff:
```python
import functools

import jax
import jax.numpy as jnp
from jax import lax
from jax.experimental import pallas as pl
from jax.experimental.pallas import tpu as pltpu
from jax.sharding import PartitionSpec as P

EPS = 1e-05
HIGH = lax.Precision.HIGHEST
MESH = pl.DeviceIdType.MESH
F32, BF16 = jnp.float32, jnp.bfloat16
EDGE = 16
STEP = 16


def from_behind(value, axis, steps):
    count = lax.axis_size(axis)
    leading, last = (max(0, -steps), min(count, count - steps))
    return lax.ppermute(value, axis, [(source, source + steps) for source in range(leading, last)])


def gelu_parts(value):
    phi = 0.5 * (1.0 + lax.erf(value * 0.7071067811865476))
    slope = phi + value * jnp.exp(-0.5 * value * value) * 0.3989422804014327
    return value * phi, slope


def dot(a, b, ca, cb, precision=None):
    return lax.dot_general(
        a, b, (((ca,), (cb,)), ((), ())), precision=precision, preferred_element_type=F32
    )


def plan(tm, rec):
    inner = [("tm", 1 << i) for i in range(1, tm.bit_length() - 1)]
    low, high = inner[: len(inner) // 2], inner[len(inner) // 2 :]
    outer = [("rec", 1 << i) for i in range(rec.bit_length() - 1)]
    core = [("tm", 1)]
    return core, [core + low + high + outer, core + high + outer + low, core + outer + low + high]


def kernel(
    tm, rec, patches_ref, taps_ref, gain_ref, bias_ref, w1_ref, w2_ref, cot_ref,
    features_ref, res_ref, small_ref,
    norm_ref, slope0_ref, act0_ref, pre1_ref, slope1_ref, act1_ref, pre2_ref, delta2_ref, delta1_ref,
    dn_ref, t0_ref, t1_ref, gf_ref, sendbuf, recvbuf, stat_ref, stat_in, little, little_in,
    rs_send, rs_recv, st_send, st_recv, sm_send, sm_recv,
):
    me = {"tm": lax.axis_index("tm"), "rec": lax.axis_index("rec")}
    rows_all, channels = norm_ref.shape[0], gain_ref.shape[1]
    rows = rows_all - EDGE
    count = 4.0 * rows * tm
    _, orders = plan(tm, rec)
    third = gf_ref.shape[0] // 3
    C = channels

    def bit_of(stage):
        axis, bit = stage
        return lax.rem(me[axis] // bit, 2)

    def partner(stage):
        axis, bit = stage
        return {axis: me[axis] + bit * (1 - 2 * bit_of(stage))}

    barrier = pltpu.get_barrier_semaphore()
    rec_bits = [s for s in orders[0] if s[0] == "rec"]
    for d in range(1, tm):
        pl.semaphore_signal(barrier, inc=1, device_id={"tm": lax.rem(me["tm"] + d, tm)}, device_id_type=MESH)
    for stage in rec_bits:
        pl.semaphore_signal(barrier, inc=1, device_id=partner(stage), device_id_type=MESH)

    for q in range(4):
        norm_ref[:, q * C : (q + 1) * C] = dot(patches_ref[q], taps_ref[...], 1, 0, HIGH)

    def sums(i, carry):
        one, two = carry
        for q in range(4):
            part = norm_ref[pl.ds(i * STEP, STEP), q * C : (q + 1) * C]
            one, two = one + part, two + part * part
        return one, two

    zero = jnp.zeros((STEP, C), F32)
    one, two = lax.fori_loop(0, rows // STEP, sums, (zero, zero))
    stat_ref[0, 0:1, :] = jnp.sum(one, 0, keepdims=True)
    stat_ref[0, 1:2, :] = jnp.sum(two, 0, keepdims=True)
    pl.semaphore_wait(barrier, tm - 1 + len(rec_bits))

    def share(which):
        copies = []
        for d in range(1, tm):
            copy = pltpu.make_async_remote_copy(
                src_ref=stat_ref.at[which],
                dst_ref=stat_in.at[which, d],
                send_sem=st_send.at[which, d],
                recv_sem=st_recv.at[which, d],
                device_id={"tm": lax.rem(me["tm"] + d, tm)},
                device_id_type=MESH,
            )
            copy.start()
            copies.append(copy)
        return copies

    def gathered(which, copies):
        total = stat_ref[which]
        for d, copy in enumerate(copies):
            copy.wait_recv()
            total = total + stat_in[which, d + 1]
        for copy in copies:
            copy.wait_send()
        return total

    total = gathered(0, share(0))
    mean = total[0:1] / count
    variance = total[1:2] / count - mean * mean
    inverse = lax.rsqrt(variance + EPS)
    gain, bias = gain_ref[...], bias_ref[...]

    def first_act(i, carry):
        at = pl.ds(pl.multiple_of(i * STEP, STEP), STEP)
        row = i * STEP + lax.broadcasted_iota(jnp.int32, (STEP, C), 0)
        past = jnp.logical_and(row == rows, me["tm"] == tm - 1)
        for q in range(4):
            lanes = slice(q * C, (q + 1) * C)
            normed = (norm_ref[at, lanes] - mean) * inverse
            norm_ref[at, lanes] = normed
            act, slope = gelu_parts(normed * gain + bias)
            act0_ref[at, lanes] = jnp.where(past, 0.0, act).astype(BF16)
            slope0_ref[at, lanes] = slope
        return carry

    lax.fori_loop(0, rows_all // STEP, first_act, 0)
    act0_ref[:, 4 * C :] = pltpu.roll(act0_ref[:, :C].astype(F32), rows_all - 1, 0).astype(BF16)

    pre1_ref[:, :C] = dot(act0_ref[:, : 3 * C], w1_ref[...], 1, 0)
    pre1_ref[:, C:] = dot(act0_ref[:, 2 * C :], w1_ref[...], 1, 0)

    def second_act(i, carry):
        at = pl.ds(pl.multiple_of(i * STEP, STEP), STEP)
        row = i * STEP + lax.broadcasted_iota(jnp.int32, (STEP, 2 * C), 0)
        past = jnp.logical_and(row == rows, me["tm"] == tm - 1)
        act, slope = gelu_parts(pre1_ref[at, :])
        act1_ref[at, : 2 * C] = jnp.where(past, 0.0, act).astype(BF16)
        slope1_ref[at, :] = slope
        return carry

    lax.fori_loop(0, rows_all // STEP, second_act, 0)
    act1_ref[:, 2 * C :] = pltpu.roll(act1_ref[:, :C].astype(F32), rows_all - 1, 0).astype(BF16)

    pre2_ref[...] = dot(act1_ref[...], w2_ref[...], 1, 0)

    def third_act(i, carry):
        at = pl.ds(pl.multiple_of(i * STEP, STEP), STEP)
        act, slope = gelu_parts(pre2_ref[at, :])
        pre2_ref[at, :] = act
        delta2_ref[at, :] = (cot_ref[at, :].astype(F32) * slope).astype(BF16)
        return carry

    lax.fori_loop(0, rows_all // STEP, third_act, 0)
    features_ref[...] = pre2_ref[:rows, :].astype(BF16)

    state = [[third, part * third, 0, []] for part in range(3)]

    def narrow(ref, source, start, size):
        block = min(32, size)

        def body(i, carry):
            at = pl.ds(pl.multiple_of(start + i * block, block), block)
            ref[at, :] = source[at, :].astype(BF16)
            return carry

        lax.fori_loop(0, size // block, body, 0)

    def launch(part):
        size, start, used, sent = state[part]
        stage = orders[part][len(sent)]
        half = size // 2 if size // 2 >= 16 else size
        bit = bit_of(stage) if half < size else 0
        keep = start + bit * half
        away = start + (1 - bit) * half if half < size else start
        narrow(sendbuf, gf_ref, away, half)
        copy = pltpu.make_async_remote_copy(
            src_ref=sendbuf.at[pl.ds(pl.multiple_of(away, 16), half), :],
            dst_ref=recvbuf.at[part, pl.ds(used, half), :],
            send_sem=rs_send.at[part, len(sent)],
            recv_sem=rs_recv.at[part, len(sent)],
            device_id=partner(stage),
            device_id_type=MESH,
        )
        copy.start()
        sent.append((copy, keep, size, start, half))

    def absorb(part):
        size, start, used, sent = state[part]
        copy, keep, _, _, half = sent[-1]
        copy.wait_recv()
        if half == size:
            copy.wait_send()
        block = min(32, half)

        def body(i, carry):
            at = pl.ds(pl.multiple_of(keep + i * block, block), block)
            came = recvbuf[part, pl.ds(pl.multiple_of(used + i * block, 16), block), :]
            gf_ref[at, :] = gf_ref[at, :] + came.astype(F32)
            return carry

        lax.fori_loop(0, half // block, body, 0)
        state[part][0], state[part][1], state[part][2] = half, keep, used + half

    gf_ref[: 3 * C, :] = dot(act1_ref[:rows, :], delta2_ref[:rows, :], 0, 0)
    launch(0)
    t0_ref[...] = dot(delta2_ref[...], w2_ref[...], 1, 1)
    even = t0_ref[:, :C] + pltpu.roll(t0_ref[:, 2 * C :], 1, 0)
    delta1_ref[:, :C] = (even * slope1_ref[:, :C]).astype(BF16)
    delta1_ref[:, C:] = (t0_ref[:, C : 2 * C] * slope1_ref[:, C:]).astype(BF16)

    gf_ref[3 * C :, :] = dot(act0_ref[:rows, : 3 * C], delta1_ref[:rows, :C], 0, 0)
    gf_ref[3 * C :, :] += dot(act0_ref[:rows, 2 * C :], delta1_ref[:rows, C:], 0, 0)
    launch(1)
    launch(2)
    absorb(0)
    launch(0)
    t0_ref[...] = dot(delta1_ref[:, :C], w1_ref[...], 1, 1)
    t1_ref[...] = dot(delta1_ref[:, C:], w1_ref[...], 1, 1)
    for part in (1, 2):
        absorb(part)
        launch(part)
    t1_ref[:, 2 * C :] = pltpu.roll(t1_ref[:, 2 * C :], 1, 0)

    def back(i, carry):
        one, two = carry
        at = pl.ds(pl.multiple_of(i * STEP, STEP), STEP)
        grads = (
            t0_ref[at, :C] + t1_ref[at, 2 * C :],
            t0_ref[at, C : 2 * C],
            t0_ref[at, 2 * C :] + t1_ref[at, :C],
            t1_ref[at, C : 2 * C],
        )
        for q in range(4):
            lanes = slice(q * C, (q + 1) * C)
            dnorm = grads[q] * slope0_ref[at, lanes]
            dn_ref[at, lanes] = dnorm
            one = one + dnorm
            two = two + dnorm * norm_ref[at, lanes]
        return one, two

    one, two = lax.fori_loop(0, rows // STEP, back, (zero, zero))
    local_one = jnp.sum(one, 0, keepdims=True)
    local_two = jnp.sum(two, 0, keepdims=True)
    stat_ref[1, 0:1, :] = local_one
    stat_ref[1, 1:2, :] = local_two
    copies = share(1)
    absorb(0)
    launch(0)
    total = gathered(1, copies)
    mean_one, mean_two = total[0:1] / count, total[1:2] / count
    scale = gain * inverse

    def through_norm(i, carry):
        at = pl.ds(pl.multiple_of(i * STEP, STEP), STEP)
        for q in range(4):
            lanes = slice(q * C, (q + 1) * C)
            dn_ref[at, lanes] = scale * (dn_ref[at, lanes] - mean_one - norm_ref[at, lanes] * mean_two)
        return carry

    lax.fori_loop(0, rows // STEP, through_norm, 0)
    grad_zero = jnp.zeros((16, C), F32)
    for q in range(4):
        grad_zero = grad_zero + dot(patches_ref[q, :rows], dn_ref[:, q * C : (q + 1) * C], 0, 0, HIGH)
    little[0] = grad_zero
    little[0, 10:11, :] = local_two
    little[0, 11:12, :] = local_one

    small_copies = []

    def launch_small():
        step = len(small_copies)
        copy = pltpu.make_async_remote_copy(
            src_ref=little.at[step],
            dst_ref=little_in.at[step],
            send_sem=sm_send.at[step],
            recv_sem=sm_recv.at[step],
            device_id=partner(orders[0][step]),
            device_id_type=MESH,
        )
        copy.start()
        small_copies.append(copy)

    def absorb_small():
        step = len(small_copies) - 1
        small_copies[-1].wait_recv()
        little[step + 1] = little[step] + little_in[step]

    stages = len(orders[0])
    launch_small()
    while min(len(s[3]) for s in state) < stages:
        for part in range(3):
            if len(state[part][3]) < stages:
                absorb(part)
                launch(part)
        if len(small_copies) < stages:
            absorb_small()
            launch_small()

    for part in range(3):
        absorb(part)
        narrow(res_ref, gf_ref, state[part][1], state[part][0])

    gathers = [[] for _ in range(3)]
    for step in range(stages - 1, -1, -1):
        for part in range(3):
            if gathers[part]:
                gathers[part][-1].wait_recv()
            _, keep, size, start, half = state[part][3][step]
            if half == size:
                continue
            piece = pl.ds(pl.multiple_of(keep, 16), half)
            copy = pltpu.make_async_remote_copy(
                src_ref=res_ref.at[piece, :],
                dst_ref=res_ref.at[piece, :],
                send_sem=rs_send.at[part, stages + step],
                recv_sem=rs_recv.at[part, stages + step],
                device_id=partner(orders[part][step]),
                device_id_type=MESH,
            )
            copy.start()
            gathers[part].append(copy)
        if len(small_copies) < stages:
            absorb_small()
            launch_small()
    while len(small_copies) < stages:
        absorb_small()
        launch_small()
    absorb_small()
    small_ref[...] = little[stages]
    for part in range(3):
        gathers[part][-1].wait_recv()
        for copy in gathers[part]:
            copy.wait_send()
        for copy, _, size, _, half in state[part][3]:
            if half < size:
                copy.wait_send()
    for copy in small_copies:
        copy.wait_send()


def shards(tm, rec, audio, conv0_weight, norm_gain, norm_bias, conv1_weight, conv2_weight, cotangent):
    samples = audio.shape[1]
    rows = samples // 20
    rows_all = rows + EDGE
    C = conv0_weight.shape[1]
    after = from_behind(audio[:, :20], "tm", -1)
    ahead = from_behind(audio[:, -20:], "tm", 1)
    cot_edge = from_behind(cotangent[0, -1:, :], "tm", 1)
    lines = jnp.concatenate(
        [audio.reshape(rows, 20), after, jnp.zeros((EDGE - 2, 20), F32), ahead], 0
    )
    wide = jnp.concatenate([lines, jnp.concatenate([lines[1:, :5], lines[:1, :5]], 0), jnp.zeros((rows_all, 6), F32)], 1)
    patches = jnp.stack([wide[:, 5 * q : 5 * q + 16] for q in range(4)], 0)
    taps = jnp.concatenate([conv0_weight, jnp.zeros((6, C), F32)], 0)
    keep = (lax.broadcasted_iota(jnp.int32, (1, 1, 16), 2) < 10).astype(F32)
    patches = patches * keep
    cot = jnp.concatenate([cotangent[0], jnp.zeros((EDGE - 1, C), BF16), cot_edge], 0)
    stages = (tm.bit_length() - 1) + (rec.bit_length() - 1)
    total_rows = 6 * C
    vmem = pl.BlockSpec(memory_space=pltpu.VMEM)
    features, res, small = pl.pallas_call(
        functools.partial(kernel, tm, rec),
        out_shape=(
            jax.ShapeDtypeStruct((rows, C), BF16),
            jax.ShapeDtypeStruct((total_rows, C), BF16),
            jax.ShapeDtypeStruct((16, C), F32),
        ),
        in_specs=[vmem] * 7,
        out_specs=(vmem,) * 3,
        scratch_shapes=[
            pltpu.VMEM((rows_all, 4 * C), F32),
            pltpu.VMEM((rows_all, 4 * C), F32),
            pltpu.VMEM((rows_all, 5 * C), BF16),
            pltpu.VMEM((rows_all, 2 * C), F32),
            pltpu.VMEM((rows_all, 2 * C), F32),
            pltpu.VMEM((rows_all, 3 * C), BF16),
            pltpu.VMEM((rows_all, C), F32),
            pltpu.VMEM((rows_all, C), BF16),
            pltpu.VMEM((rows_all, 2 * C), BF16),
            pltpu.VMEM((rows, 4 * C), F32),
            pltpu.VMEM((rows_all, 3 * C), F32),
            pltpu.VMEM((rows_all, 3 * C), F32),
            pltpu.VMEM((total_rows, C), F32),
            pltpu.VMEM((total_rows, C), BF16),
            pltpu.VMEM((3, total_rows // 3 + 64, C), BF16),
            pltpu.VMEM((2, 2, C), F32),
            pltpu.VMEM((2, tm, 2, C), F32),
            pltpu.VMEM((stages + 1, 16, C), F32),
            pltpu.VMEM((stages, 16, C), F32),
            pltpu.SemaphoreType.DMA((3, 2 * stages)),
            pltpu.SemaphoreType.DMA((3, 2 * stages)),
            pltpu.SemaphoreType.DMA((2, tm)),
            pltpu.SemaphoreType.DMA((2, tm)),
            pltpu.SemaphoreType.DMA((stages,)),
            pltpu.SemaphoreType.DMA((stages,)),
        ],
        compiler_params=pltpu.CompilerParams(
            collective_id=0, has_side_effects=True, vmem_limit_bytes=52 * 2**20
        ),
    )(patches, taps, norm_gain[None, :], norm_bias[None, :], conv1_weight, conv2_weight, cot)
    grad_two = res[: 3 * C].astype(F32)
    grad_one = res[3 * C :].astype(F32)
    return (features[None], small[:10], small[10], small[11], grad_one, grad_two)


def solution(mesh):
    return jax.shard_map(
        functools.partial(shards, mesh.shape["tm"], mesh.shape["rec"]),
        mesh=mesh,
        in_specs=(P("rec", "tm"), P(), P(), P(), P(), P(), P("rec", "tm", None)),
        out_specs=(P("rec", "tm", None), P(), P(), P(), P(), P()),
        check_vma=False,
    )
```

time: 251 us -> 94.7 us (0.38)
  waiting for transfers between devices: 84.2 us -> 0.01 us
  Pallas kernels: 0 us -> 71.9 us
  blocking collectives: 70.5 us -> 0 us
  matrix products: 24.5 us -> 0 us
  other arithmetic: 25.2 us -> 7.39 us
  local copies, waits for them, and re-layouts: 19.4 us -> 5.5 us
  between operations: 14.3 us -> 0.8 us
  starting transfers between devices: 11.5 us -> 8.75 us
    psum x1 -> x0, waiting for transfers between devices: 82.8 us -> none  [shards(): lax.psum((grad_zero, norm_terms, grad_one, grad_two), ('rec', 'tm'))]
    pallas_call x0 -> x1, Pallas kernels: none -> 71.9 us  [shards(): pl.pallas_call(functools.partial(kernel, tm, rec), out_shape=(jax.ShapeDt...]
    psum x3 -> x0, blocking collectives: 70.5 us -> none  [the longest x1 42.1 us: shards(): lax.psum((grad_zero, norm_terms, grad_one, grad_two), ('rec', 'tm'))]
    dot_general x14 -> x0, matrix products: 24.5 us -> none  [the longest x2 7.41 us: stride_conv(): jnp.einsum('rtk,kc->rtc', following, weight[2 * channels:], preferred_ele...]
    convert_element_type x4 -> x2, other arithmetic: 14.5 us -> 5.48 us  [the longest x1 5.48 us: shards(): grad_two = res[:3 * C].astype(F32)]
    reshape x6 -> x2, local copies, waits for them, and re-layouts: 6.59 us -> 0.22 us  [shards(): audio.reshape(rows, 20)]
    unnamed x23 -> x9, local copies, waits for them, and re-layouts: 7.54 us -> 1.84 us
    concatenate x5 -> x3, other arithmetic: 5.59 us -> 0.28 us  [the longest x1 0.12 us: shards(): jnp.concatenate([cotangent[0], jnp.zeros((EDGE - 1, C), BF16), cot_edge], 0)]
  transfers between devices with their start and end apart: 6 -> 3, of which waited for: 2 -> 0; matrix products, arithmetic and copies ran while one was open for 12% -> 5% of each run, Pallas kernels for 0% -> 0%
where the time goes in v1:
time: 94.7 us; the launch traced here: 94.4 us
  Pallas kernels  71.9 us (76%)
  starting transfers between devices  8.75 us (9%)
  other arithmetic  7.39 us (8%)
  local copies, waits for them, and re-layouts  5.5 us (6%)
    pallas_call x1, Pallas kernels, shards(): pl.pallas_call(functools.partial(kernel, tm, rec), out_shape=(jax.ShapeDt...  71.9 us
    ppermute x3, starting transfers between devices, from_behind(): lax.ppermute(value, axis, [(source, source + steps) for source in range(l...  8.75 us
    convert_element_type x1, other arithmetic, shards(): grad_two = res[:3 * C].astype(F32)  5.48 us
  transfers between devices with their start and end apart: 3, of which 0 were waited for; matrix products, arithmetic and copies ran while one was open for 5% of the time, Pallas kernels for 0%

profile of v1, /device:TPU:0, one launch (start us, length us, event | category | flops | bytes accessed | tf_op | source)
XLA Modules:
  0.0 94.4 jit_solution(12051984528738714974)
XLA Ops:
  0.6 0.0 copy-start.2
  0.6 0.0 copy-start
  0.7 0.0 copy-start.1
  0.7 0.8 fusion.3
  1.4 0.1 copy.18
  1.5 1.3 %collective-permute-start = (f32[1,20]{0,1:T(8,128)S(1)}, f32[1,20]{0,1:T(8,128)S(1)}, u32[]{:S(2)}, u32[]{:S(2)}) collective-permute-start(f32[1,20]{0,1:T(8,128)S(1)} %copy.18), channel_id=1, source_target_pairs={{1,0},{2,1},{3,2},{4,3},{5,4},{6,5},{7,6},{9,8},{10,9},{11,10},{12... | collective-permute-start | bytes 248 | tf_op jit(solution)/shard_map/ppermute | solution.py:21
  2.8 0.1 copy.19
  2.9 3.0 %collective-permute-start.1 = (f32[1,20]{0,1:T(8,128)S(1)}, f32[1,20]{0,1:T(8,128)S(1)}, u32[]{:S(2)}, u32[]{:S(2)}) collective-permute-start(f32[1,20]{0,1:T(8,128)S(1)} %copy.19), channel_id=1, source_target_pairs={{0,1},{1,2},{2,3},{3,4},{4,5},{5,6},{6,7},{8,9},{9,10},{10,11},{11... | collective-permute-start | bytes 248 | tf_op jit(solution)/shard_map/ppermute | solution.py:21
  6.0 0.7 slice_bitcast_fusion.3
  6.7 4.5 %collective-permute-start.2 = (bf16[1,512]{1,0:T(2,128)(2,1)S(1)}, bf16[1,512]{1,0:T(2,128)(2,1)S(1)}, u32[]{:S(2)}, u32[]{:S(2)}) collective-permute-start(bf16[1,512]{1,0:T(2,128)(2,1)S(1)} %slice_bitcast_fusion.3), channel_id=1, source_target_pairs={{0,1},{1,2},{2,3},{3,4},{4,5},{5,6},{6,7},{8,9},{9,10},{10,11},{11... | collective-permute-start | bytes 3080 | tf_op jit(solution)/shard_map/ppermute | solution.py:21
  11.1 0.5 broadcast.19
  11.6 1.4 %reduce.3 = f32[5120]{0:T(1024)S(1)} reduce(f32[1,5120]{1,0:T(1,128)} %param.7, f32[]{:T(128)} %broadcast.19), dimensions={0}, to_apply=%param.7.reduce_sub_computation.3 | reduce | bytes 40964 | tf_op args[0]
  13.1 0.1 reshape.22
  13.2 0.1 copy.20
  13.3 0.1 copy.21
  13.4 0.8 concatenate.22.taps_ref
  14.2 0.1 pad.14.clone
  14.3 0.0 collective-permute-done
  14.3 0.0 collective-permute-done.1
  14.3 0.1 pad_maximum_fusion.2
  14.4 0.1 pad_maximum_fusion.7
  14.5 0.1 maximum_maximum_fusion
  14.5 0.1 slice_bitcast_fusion.1
  14.6 0.2 copy.22
  14.9 0.0 collective-permute-done.2
  14.9 0.0 copy-done.2
  14.9 0.1 pad_maximum_fusion.cot_ref
  15.0 0.0 copy-done
  15.1 0.0 copy-done.1
  15.1 71.9 %shard_map.118 = (bf16[256,512]{1,0:T(8,128)(2,1)S(1)}, bf16[3072,512]{1,0:T(8,128)(2,1)}, f32[16,512]{1,0:T(8,128)S(1)}) custom-call(f32[4,272,16]{2,1,0:T(8,128)S(1)} %broadcast_multiply_fusion.patches_ref, f32[16,512]{1,0:T(8,128)S(1)} %concatenate.22.taps_ref, f32[1,512]{1,0:T(1,128)S(1)} %bitcast.19, f32[1,512]{1,0:T(1,128)S(1)} %bitcast.20, ...), custom_call_target="tpu_custom_call" | custom-call | tf_op jit(solution)/shard_map/pallas_call | solution.py:368
  87.0 5.5 %slice_convert_fusion = (f32[1536,512]{1,0:T(8,128)}, f32[1536,512]{1,0:T(8,128)}) fusion(bf16[3072,512]{1,0:T(8,128)(2,1)} %get-tuple-element.11), kind=kLoop, calls=%fused_computation | loop fusion | flops 1572864 | bytes 9437184 | tf_op jit(solution)/shard_map/convert_element_type | solution.py:408
  92.4 0.6 fusion.2
  93.0 0.7 copy.26
  93.7 0.6 copy.27
  (9 shorter events, 0.1 us)
Async XLA Ops:
  0.6 14.3 %copy-start.2 = (bf16[1,256,512]{2,1,0:T(8,128)(2,1)S(1)}, bf16[1,256,512]{2,1,0:T(8,128)(2,1)}, u32[]{:S(2)}) copy-start(bf16[1,256,512]{2,1,0:T(8,128)(2,1)} %param.13) | copy-start | bytes 786436
  0.6 14.4 %copy-start = (f32[512]{0:T(512)S(1)}, f32[512]{0:T(512)}, u32[]{:S(2)}) copy-start(f32[512]{0:T(512)} %param.9) | copy-start | bytes 6148
  0.7 14.4 %copy-start.1 = (f32[512]{0:T(512)S(1)}, f32[512]{0:T(512)}, u32[]{:S(2)}) copy-start(f32[512]{0:T(512)} %param.10) | copy-start | bytes 6148
  1.5 12.7 %collective-permute-start = (f32[1,20]{0,1:T(8,128)S(1)}, f32[1,20]{0,1:T(8,128)S(1)}, u32[]{:S(2)}, u32[]{:S(2)}) collective-permute-start(f32[1,20]{0,1:T(8,128)S(1)} %copy.18), channel_id=1, source_target_pairs={{1,0},{2,1},{3,2},{4,3},{5,4},{6,5},{7,6},{9,8},{10,9},{11,10},{12... | collective-permute-start | bytes 248 | tf_op jit(solution)/shard_map/ppermute | solution.py:21
  2.9 11.3 %collective-permute-start.1 = (f32[1,20]{0,1:T(8,128)S(1)}, f32[1,20]{0,1:T(8,128)S(1)}, u32[]{:S(2)}, u32[]{:S(2)}) collective-permute-start(f32[1,20]{0,1:T(8,128)S(1)} %copy.19), channel_id=1, source_target_pairs={{0,1},{1,2},{2,3},{3,4},{4,5},{5,6},{6,7},{8,9},{9,10},{10,11},{11... | collective-permute-start | bytes 248 | tf_op jit(solution)/shard_map/ppermute | solution.py:21
  6.7 8.2 %collective-permute-start.2 = (bf16[1,512]{1,0:T(2,128)(2,1)S(1)}, bf16[1,512]{1,0:T(2,128)(2,1)S(1)}, u32[]{:S(2)}, u32[]{:S(2)}) collective-permute-start(bf16[1,512]{1,0:T(2,128)(2,1)S(1)} %slice_bitcast_fusion.3), channel_id=1, source_target_pairs={{0,1},{1,2},{2,3},{3,4},{4,5},{5,6},{6,7},{8,9},{9,10},{10,11},{11... | collective-permute-start | bytes 3080 | tf_op jit(solution)/shard_map/ppermute | solution.py:21

commit v2 on v1

--- a/solution.py
+++ b/solution.py
@@ -15,12 +15,6 @@
 STEP = 16
 
 
-def from_behind(value, axis, steps):
-    count = lax.axis_size(axis)
-    leading, last = (max(0, -steps), min(count, count - steps))
-    return lax.ppermute(value, axis, [(source, source + steps) for source in range(leading, last)])
-
-
 def gelu_parts(value):
     phi = 0.5 * (1.0 + lax.erf(value * 0.7071067811865476))
     slope = phi + value * jnp.exp(-0.5 * value * value) * 0.3989422804014327
@@ -38,22 +32,24 @@
     low, high = inner[: len(inner) // 2], inner[len(inner) // 2 :]
     outer = [("rec", 1 << i) for i in range(rec.bit_length() - 1)]
     core = [("tm", 1)]
-    return core, [core + low + high + outer, core + high + outer + low, core + outer + low + high]
+    one, two = core + low + high + outer, core + high + low + outer
+    return [one, two, core + outer + low + high, one, two, core + outer + high + low]
 
 
 def kernel(
-    tm, rec, patches_ref, taps_ref, gain_ref, bias_ref, w1_ref, w2_ref, cot_ref,
+    tm, rec, audio_ref, taps_ref, gain_ref, bias_ref, w1_ref, w2_ref, cot_ref,
     features_ref, res_ref, small_ref,
     norm_ref, slope0_ref, act0_ref, pre1_ref, slope1_ref, act1_ref, pre2_ref, delta2_ref, delta1_ref,
-    dn_ref, t0_ref, t1_ref, gf_ref, sendbuf, recvbuf, stat_ref, stat_in, little, little_in,
-    rs_send, rs_recv, st_send, st_recv, sm_send, sm_recv,
+    x_ref, xx_ref, wide_ref, edge_ref, dn_ref, t0_ref, t1_ref, gf_ref, sendbuf, recvbuf, stat_ref, stat_in, little, little_in,
+    ed_send, ed_recv, rs_send, rs_recv, st_send, st_recv, sm_send, sm_recv,
 ):
     me = {"tm": lax.axis_index("tm"), "rec": lax.axis_index("rec")}
     rows_all, channels = norm_ref.shape[0], gain_ref.shape[1]
     rows = rows_all - EDGE
     count = 4.0 * rows * tm
-    _, orders = plan(tm, rec)
-    third = gf_ref.shape[0] // 3
+    orders = plan(tm, rec)
+    stages, parts = len(orders[0]), len(orders)
+    share_rows = gf_ref.shape[0] // parts
     C = channels
 
     def bit_of(stage):
@@ -71,8 +67,39 @@
     for stage in rec_bits:
         pl.semaphore_signal(barrier, inc=1, device_id=partner(stage), device_id_type=MESH)
 
+    x_ref[:rows, :] = audio_ref[...]
     for q in range(4):
-        norm_ref[:, q * C : (q + 1) * C] = dot(patches_ref[q], taps_ref[...], 1, 0, HIGH)
+        wide = taps_ref[...] if q == 0 else pltpu.roll(taps_ref[...], 5 * q, 0)
+        wide_ref[:, q * C : (q + 1) * C] = wide
+    pl.semaphore_wait(barrier, tm - 1 + len(rec_bits))
+    behind, ahead = lax.rem(me["tm"] + 1, tm), lax.rem(me["tm"] + tm - 1, tm)
+    edges = []
+    for i, (source, target, device) in enumerate((
+        (x_ref.at[0:8, :], x_ref.at[rows : rows + 8, :], ahead),
+        (x_ref.at[rows - 8 : rows, :], x_ref.at[rows + 8 : rows + 16, :], behind),
+        (cot_ref.at[rows - 16 : rows, :], edge_ref, behind),
+    )):
+        copy = pltpu.make_async_remote_copy(
+            src_ref=source, dst_ref=target, send_sem=ed_send.at[i], recv_sem=ed_recv.at[i],
+            device_id={"tm": device}, device_id_type=MESH,
+        )
+        copy.start()
+        edges.append(copy)
+    for copy in edges:
+        copy.wait()
+
+    row = lax.broadcasted_iota(jnp.int32, x_ref.shape, 0)
+    lane = lax.broadcasted_iota(jnp.int32, x_ref.shape, 1)
+    outside = jnp.logical_or(
+        jnp.logical_and(row >= rows + 8, me["tm"] == 0),
+        jnp.logical_and(jnp.logical_and(row >= rows, row < rows + 8), me["tm"] == tm - 1),
+    )
+    x = jnp.where(outside, 0.0, x_ref[...])
+    next_row = jnp.where(lane < 5, pltpu.roll(x, rows_all - 1, 0), 0.0)
+    xx_ref[...] = x + pltpu.roll(next_row, 20, 1)
+    for q in range(4):
+        lanes = slice(q * C, (q + 1) * C)
+        norm_ref[:, lanes] = dot(xx_ref[:, :32], wide_ref[:, lanes], 1, 0, HIGH)
 
     def sums(i, carry):
         one, two = carry
@@ -85,7 +112,6 @@
     one, two = lax.fori_loop(0, rows // STEP, sums, (zero, zero))
     stat_ref[0, 0:1, :] = jnp.sum(one, 0, keepdims=True)
     stat_ref[0, 1:2, :] = jnp.sum(two, 0, keepdims=True)
-    pl.semaphore_wait(barrier, tm - 1 + len(rec_bits))
 
     def share(which):
         copies = []
@@ -153,79 +179,103 @@
     def third_act(i, carry):
         at = pl.ds(pl.multiple_of(i * STEP, STEP), STEP)
         act, slope = gelu_parts(pre2_ref[at, :])
-        pre2_ref[at, :] = act
+        features_ref[at, :] = act.astype(BF16)
         delta2_ref[at, :] = (cot_ref[at, :].astype(F32) * slope).astype(BF16)
         return carry
 
-    lax.fori_loop(0, rows_all // STEP, third_act, 0)
-    features_ref[...] = pre2_ref[:rows, :].astype(BF16)
-
-    state = [[third, part * third, 0, []] for part in range(3)]
-
-    def narrow(ref, source, start, size):
+    lax.fori_loop(0, rows // STEP, third_act, 0)
+    slope = gelu_parts(pre2_ref[rows:, :])[1]
+    edge = jnp.where(me["tm"] == 0, 0.0, edge_ref[...].astype(F32))
+    delta2_ref[rows:, :] = (edge * slope).astype(BF16)
+
+    state = [{"size": share_rows, "start": p * share_rows, "used": 0, "step": 0, "sent": [], "back": []} for p in range(parts)]
+
+    def combine(target, part, start, size, came_at):
         block = min(32, size)
 
         def body(i, carry):
-            at = pl.ds(pl.multiple_of(start + i * block, block), block)
-            ref[at, :] = source[at, :].astype(BF16)
+            at = pl.ds(pl.multiple_of(start + i * block, 16), block)
+            value = gf_ref[at, :]
+            if came_at is not None:
+                value = value + recvbuf[part, pl.ds(pl.multiple_of(came_at + i * block, 16), block), :].astype(F32)
+            target[at, :] = value.astype(target.dtype)
             return carry
 
         lax.fori_loop(0, size // block, body, 0)
 
-    def launch(part):
-        size, start, used, sent = state[part]
-        stage = orders[part][len(sent)]
-        half = size // 2 if size // 2 >= 16 else size
-        bit = bit_of(stage) if half < size else 0
-        keep = start + bit * half
-        away = start + (1 - bit) * half if half < size else start
-        narrow(sendbuf, gf_ref, away, half)
+    def send_piece(part, ref_from, ref_to, index, stage):
         copy = pltpu.make_async_remote_copy(
-            src_ref=sendbuf.at[pl.ds(pl.multiple_of(away, 16), half), :],
-            dst_ref=recvbuf.at[part, pl.ds(used, half), :],
-            send_sem=rs_send.at[part, len(sent)],
-            recv_sem=rs_recv.at[part, len(sent)],
-            device_id=partner(stage),
-            device_id_type=MESH,
+            src_ref=ref_from, dst_ref=ref_to,
+            send_sem=rs_send.at[part, index], recv_sem=rs_recv.at[part, index],
+            device_id=partner(stage), device_id_type=MESH,
         )
         copy.start()
-        sent.append((copy, keep, size, start, half))
-
-    def absorb(part):
-        size, start, used, sent = state[part]
-        copy, keep, _, _, half = sent[-1]
-        copy.wait_recv()
-        if half == size:
-            copy.wait_send()
-        block = min(32, half)
-
-        def body(i, carry):
-            at = pl.ds(pl.multiple_of(keep + i * block, block), block)
-            came = recvbuf[part, pl.ds(pl.multiple_of(used + i * block, 16), block), :]
-            gf_ref[at, :] = gf_ref[at, :] + came.astype(F32)
-            return carry
-
-        lax.fori_loop(0, half // block, body, 0)
-        state[part][0], state[part][1], state[part][2] = half, keep, used + half
+        return copy
+
+    def advance(part):
+        s = state[part]
+        step, size, start = s["step"], s["size"], s["start"]
+        s["step"] += 1
+        if step <= stages:
+            base = None
+            if step > 0:
+                last, _, _, last_half, whole = s["sent"][-1]
+                last.wait_recv()
+                if whole:
+                    last.wait_send()
+                base = s["used"] - last_half
+        if step < stages:
+            stage = orders[part][step]
+            whole = size // 2 < 16
+            if whole:
+                half, keep, away = size, start, start
+                if base is not None:
+                    combine(gf_ref, part, start, size, base)
+                combine(sendbuf, part, start, size, None)
+            else:
+                half, bit = size // 2, bit_of(stage)
+                keep, away = start + bit * half, start + (1 - bit) * half
+                combine(sendbuf, part, away, half, None if base is None else base + (1 - bit) * half)
+            copy = send_piece(
+                part,
+                sendbuf.at[pl.ds(pl.multiple_of(away, 16), half), :],
+                recvbuf.at[part, pl.ds(s["used"], half), :],
+                step, stage,
+            )
+            if not whole and base is not None:
+                combine(gf_ref, part, keep, half, base + bit * half)
+            s["sent"].append((copy, keep, size, half, whole))
+            s["size"], s["start"], s["used"] = half, keep, s["used"] + half
+            return
+        if step == stages:
+            combine(res_ref, part, start, size, base)
+        elif s["back"]:
+            s["back"][-1].wait_recv()
+        index = 2 * stages - 1 - step
+        if index >= 0:
+            _, keep, _, half, whole = s["sent"][index]
+            if not whole:
+                piece = res_ref.at[pl.ds(pl.multiple_of(keep, 16), half), :]
+                s["back"].append(send_piece(part, piece, piece, stages + index, orders[part][index]))
 
     gf_ref[: 3 * C, :] = dot(act1_ref[:rows, :], delta2_ref[:rows, :], 0, 0)
-    launch(0)
+    for part in (0, 1, 2):
+        advance(part)
     t0_ref[...] = dot(delta2_ref[...], w2_ref[...], 1, 1)
     even = t0_ref[:, :C] + pltpu.roll(t0_ref[:, 2 * C :], 1, 0)
     delta1_ref[:, :C] = (even * slope1_ref[:, :C]).astype(BF16)
     delta1_ref[:, C:] = (t0_ref[:, C : 2 * C] * slope1_ref[:, C:]).astype(BF16)
+    for part in (0, 1, 2):
+        advance(part)
 
     gf_ref[3 * C :, :] = dot(act0_ref[:rows, : 3 * C], delta1_ref[:rows, :C], 0, 0)
     gf_ref[3 * C :, :] += dot(act0_ref[:rows, 2 * C :], delta1_ref[:rows, C:], 0, 0)
-    launch(1)
-    launch(2)
-    absorb(0)
-    launch(0)
+    for part in (3, 4, 5):
+        advance(part)
     t0_ref[...] = dot(delta1_ref[:, :C], w1_ref[...], 1, 1)
     t1_ref[...] = dot(delta1_ref[:, C:], w1_ref[...], 1, 1)
-    for part in (1, 2):
-        absorb(part)
-        launch(part)
+    for part in (0, 3, 1, 4, 2, 5):
+        advance(part)
     t1_ref[:, 2 * C :] = pltpu.roll(t1_ref[:, 2 * C :], 1, 0)
 
     def back(i, carry):
@@ -251,8 +301,8 @@
     stat_ref[1, 0:1, :] = local_one
     stat_ref[1, 1:2, :] = local_two
     copies = share(1)
-    absorb(0)
-    launch(0)
+    for part in (0, 1, 2):
+        advance(part)
     total = gathered(1, copies)
     mean_one, mean_two = total[0:1] / count, total[1:2] / count
     scale = gain * inverse
@@ -265,10 +315,13 @@
         return carry
 
     lax.fori_loop(0, rows // STEP, through_norm, 0)
-    grad_zero = jnp.zeros((16, C), F32)
+    for part in (3, 4, 5):
+        advance(part)
+    grad_zero = jnp.zeros((32, C), F32)
     for q in range(4):
-        grad_zero = grad_zero + dot(patches_ref[q, :rows], dn_ref[:, q * C : (q + 1) * C], 0, 0, HIGH)
-    little[0] = grad_zero
+        taps = dot(xx_ref[:rows, :32], dn_ref[:, q * C : (q + 1) * C], 0, 0, HIGH)
+        grad_zero = grad_zero + (taps if q == 0 else pltpu.roll(taps, 32 - 5 * q, 0))
+    little[0] = grad_zero[:16]
     little[0, 10:11, :] = local_two
     little[0, 11:12, :] = local_one
 
@@ -292,40 +345,11 @@
         small_copies[-1].wait_recv()
         little[step + 1] = little[step] + little_in[step]
 
-    stages = len(orders[0])
     launch_small()
-    while min(len(s[3]) for s in state) < stages:
-        for part in range(3):
-            if len(state[part][3]) < stages:
-                absorb(part)
-                launch(part)
-        if len(small_copies) < stages:
-            absorb_small()
-            launch_small()
-
-    for part in range(3):
-        absorb(part)
-        narrow(res_ref, gf_ref, state[part][1], state[part][0])
-
-    gathers = [[] for _ in range(3)]
-    for step in range(stages - 1, -1, -1):
-        for part in range(3):
-            if gathers[part]:
-                gathers[part][-1].wait_recv()
-            _, keep, size, start, half = state[part][3][step]
-            if half == size:
-                continue
-            piece = pl.ds(pl.multiple_of(keep, 16), half)
-            copy = pltpu.make_async_remote_copy(
-                src_ref=res_ref.at[piece, :],
-                dst_ref=res_ref.at[piece, :],
-                send_sem=rs_send.at[part, stages + step],
-                recv_sem=rs_recv.at[part, stages + step],
-                device_id=partner(orders[part][step]),
-                device_id_type=MESH,
-            )
-            copy.start()
-            gathers[part].append(copy)
+    while min(s["step"] for s in state) <= 2 * stages:
+        for part in range(parts):
+            if state[part]["step"] <= 2 * stages:
+                advance(part)
         if len(small_copies) < stages:
             absorb_small()
             launch_small()
@@ -334,12 +358,11 @@
         launch_small()
     absorb_small()
     small_ref[...] = little[stages]
-    for part in range(3):
-        gathers[part][-1].wait_recv()
-        for copy in gathers[part]:
+    for s in state:
+        for copy in s["back"]:
             copy.wait_send()
-        for copy, _, size, _, half in state[part][3]:
-            if half < size:
+        for copy, _, _, _, whole in s["sent"]:
+            if not whole:
                 copy.wait_send()
     for copy in small_copies:
         copy.wait_send()
@@ -350,18 +373,8 @@
     rows = samples // 20
     rows_all = rows + EDGE
     C = conv0_weight.shape[1]
-    after = from_behind(audio[:, :20], "tm", -1)
-    ahead = from_behind(audio[:, -20:], "tm", 1)
-    cot_edge = from_behind(cotangent[0, -1:, :], "tm", 1)
-    lines = jnp.concatenate(
-        [audio.reshape(rows, 20), after, jnp.zeros((EDGE - 2, 20), F32), ahead], 0
-    )
-    wide = jnp.concatenate([lines, jnp.concatenate([lines[1:, :5], lines[:1, :5]], 0), jnp.zeros((rows_all, 6), F32)], 1)
-    patches = jnp.stack([wide[:, 5 * q : 5 * q + 16] for q in range(4)], 0)
-    taps = jnp.concatenate([conv0_weight, jnp.zeros((6, C), F32)], 0)
-    keep = (lax.broadcasted_iota(jnp.int32, (1, 1, 16), 2) < 10).astype(F32)
-    patches = patches * keep
-    cot = jnp.concatenate([cotangent[0], jnp.zeros((EDGE - 1, C), BF16), cot_edge], 0)
+    lines = jnp.pad(audio.reshape(rows, 20), ((0, 0), (0, 108)))
+    taps = jnp.concatenate([conv0_weight, jnp.zeros((22, C), F32)], 0)
     stages = (tm.bit_length() - 1) + (rec.bit_length() - 1)
     total_rows = 6 * C
     vmem = pl.BlockSpec(memory_space=pltpu.VMEM)
@@ -384,18 +397,24 @@
             pltpu.VMEM((rows_all, C), F32),
             pltpu.VMEM((rows_all, C), BF16),
             pltpu.VMEM((rows_all, 2 * C), BF16),
+            pltpu.VMEM((rows_all, 128), F32),
+            pltpu.VMEM((rows_all, 128), F32),
+            pltpu.VMEM((32, 4 * C), F32),
+            pltpu.VMEM((EDGE, C), BF16),
             pltpu.VMEM((rows, 4 * C), F32),
             pltpu.VMEM((rows_all, 3 * C), F32),
             pltpu.VMEM((rows_all, 3 * C), F32),
             pltpu.VMEM((total_rows, C), F32),
             pltpu.VMEM((total_rows, C), BF16),
-            pltpu.VMEM((3, total_rows // 3 + 64, C), BF16),
+            pltpu.VMEM((6, total_rows // 6 + 96, C), BF16),
             pltpu.VMEM((2, 2, C), F32),
             pltpu.VMEM((2, tm, 2, C), F32),
             pltpu.VMEM((stages + 1, 16, C), F32),
             pltpu.VMEM((stages, 16, C), F32),
-            pltpu.SemaphoreType.DMA((3, 2 * stages)),
-            pltpu.SemaphoreType.DMA((3, 2 * stages)),
+            pltpu.SemaphoreType.DMA((3,)),
+            pltpu.SemaphoreType.DMA((3,)),
+            pltpu.SemaphoreType.DMA((6, 2 * stages)),
+            pltpu.SemaphoreType.DMA((6, 2 * stages)),
             pltpu.SemaphoreType.DMA((2, tm)),
             pltpu.SemaphoreType.DMA((2, tm)),
             pltpu.SemaphoreType.DMA((stages,)),
@@ -404,7 +423,7 @@
         compiler_params=pltpu.CompilerParams(
             collective_id=0, has_side_effects=True, vmem_limit_bytes=52 * 2**20
         ),
-    )(patches, taps, norm_gain[None, :], norm_bias[None, :], conv1_weight, conv2_weight, cot)
+    )(lines, taps, norm_gain[None, :], norm_bias[None, :], conv1_weight, conv2_weight, cotangent[0])
     grad_two = res[: 3 * C].astype(F32)
     grad_one = res[3 * C :].astype(F32)
     return (features[None], small[:10], small[10], small[11], grad_one, grad_two)

time: 94.7 us -> 78 us (0.82)
  starting transfers between devices: 8.75 us -> 0 us
  Pallas kernels: 71.9 us -> 64.4 us
    ppermute x3 -> x0, starting transfers between devices: 8.75 us -> none  [from_behind(): lax.ppermute(value, axis, [(source, source + steps) for source in range(l...]
    pallas_call x1, Pallas kernels: 71.9 us -> 64.4 us  [shards(): pl.pallas_call(functools.partial(kernel, tm, rec), out_shape=(jax.ShapeDt...]
    unnamed x9, local copies, waits for them, and re-layouts: 1.84 us -> 4.14 us
    slice x5 -> x0, local copies, waits for them, and re-layouts: 1.07 us -> none  [the longest x2 0.88 us: shards(): after = from_behind(audio[:, :20], 'tm', -1)]
  transfers between devices with their start and end apart: 3 -> 0, of which waited for: 0 -> 0; matrix products, arithmetic and copies ran while one was open for 5% -> 0% of each run, Pallas kernels for 0% -> 0%
where the time goes in v2:
time: 78 us; the launch traced here: 77.6 us
  Pallas kernels  64.4 us (83%)
  other arithmetic  6.9 us (9%)
  local copies, waits for them, and re-layouts  5.65 us (7%)
    pallas_call x1, Pallas kernels, shards(): pl.pallas_call(functools.partial(kernel, tm, rec), out_shape=(jax.ShapeDt...  64.4 us
    convert_element_type x1, other arithmetic, shards(): grad_two = res[:3 * C].astype(F32)  5.48 us
    unnamed x9, local copies, waits for them, and re-layouts  4.14 us

profile of v2, /device:TPU:0, one launch (start us, length us, event | category | flops | bytes accessed | tf_op | source)
XLA Modules:
  0.0 77.6 jit_solution(16206068969029238100)
XLA Ops:
  0.6 0.5 broadcast.7
  1.1 1.4 %reduce.3 = f32[5120]{0:T(1024)S(1)} reduce(f32[1,5120]{1,0:T(1,128)} %param.7, f32[]{:T(128)} %broadcast.7), dimensions={0}, to_apply=%param.7.reduce_sub_computation.3 | reduce | bytes 40964 | tf_op args[0]
  2.6 0.8 concatenate.3.taps_ref
  3.3 0.1 reshape.15
  3.5 0.0 copy-start
  3.5 0.9 %copy-done = bf16[1,256,512]{2,1,0:T(8,128)(2,1)S(1)} copy-done((bf16[1,256,512]{2,1,0:T(8,128)(2,1)S(1)}, bf16[1,256,512]{2,1,0:T(8,128)(2,1)}, u32[]{:S(2)}) %copy-start) | copy-done | bytes 262168
  4.5 0.0 copy-start.1
  4.5 0.7 copy-done.1
  5.1 0.0 copy-start.2
  5.1 0.7 copy-done.2
  5.8 64.4 %shard_map.118 = (bf16[256,512]{1,0:T(8,128)(2,1)S(1)}, bf16[3072,512]{1,0:T(8,128)(2,1)}, f32[16,512]{1,0:T(8,128)S(1)}) custom-call(f32[256,128]{1,0:T(8,128)S(1)} %pad.5.audio_ref, f32[32,512]{1,0:T(8,128)S(1)} %concatenate.3.taps_ref, f32[1,512]{1,0:T(1,128)S(1)} %bitcast.10, f32[1,512]{1,0:T(1,128)S(1)} %bitcast.11, bf16[1536,512]{1,0:T(8,128)(2,1)} %w1_ref.1, ...), custom_call_target="tpu_custom_call" | custom-call | tf_op jit(solution)/shard_map/pallas_call | solution.py:381
  70.3 0.6 fusion
  70.8 5.5 %slice_convert_fusion = (f32[1536,512]{1,0:T(8,128)}, f32[1536,512]{1,0:T(8,128)}) fusion(bf16[3072,512]{1,0:T(8,128)(2,1)} %get-tuple-element.11), kind=kLoop, calls=%fused_computation | loop fusion | flops 1572864 | bytes 9437184 | tf_op jit(solution)/shard_map/convert_element_type | solution.py:427
  76.3 0.7 copy.15
  77.0 0.6 copy.16
  (1 shorter events, 0.0 us)
Async XLA Ops:
  3.5 1.0 %copy-start = (bf16[1,256,512]{2,1,0:T(8,128)(2,1)S(1)}, bf16[1,256,512]{2,1,0:T(8,128)(2,1)}, u32[]{:S(2)}) copy-start(bf16[1,256,512]{2,1,0:T(8,128)(2,1)} %param.13) | copy-start | bytes 786436
  4.5 0.7 copy-start.1
  5.1 0.7 copy-start.2

commit v3 on v2

--- a/solution.py
+++ b/solution.py
@@ -37,11 +37,11 @@
 
 
 def kernel(
-    tm, rec, audio_ref, taps_ref, gain_ref, bias_ref, w1_ref, w2_ref, cot_ref,
+    tm, rec, audio_ref, taps_ref, gain_ref, bias_ref, w1_hbm, w2_hbm, cot_ref,
     features_ref, res_ref, small_ref,
     norm_ref, slope0_ref, act0_ref, pre1_ref, slope1_ref, act1_ref, pre2_ref, delta2_ref, delta1_ref,
     x_ref, xx_ref, wide_ref, edge_ref, dn_ref, t0_ref, t1_ref, gf_ref, sendbuf, recvbuf, stat_ref, stat_in, little, little_in,
-    ed_send, ed_recv, rs_send, rs_recv, st_send, st_recv, sm_send, sm_recv,
+    w1_ref, w2_ref, load_sem, ed_send, ed_recv, rs_send, rs_recv, st_send, st_recv, sm_send, sm_recv,
 ):
     me = {"tm": lax.axis_index("tm"), "rec": lax.axis_index("rec")}
     rows_all, channels = norm_ref.shape[0], gain_ref.shape[1]
@@ -60,6 +60,12 @@
         axis, bit = stage
         return {axis: me[axis] + bit * (1 - 2 * bit_of(stage))}
 
+    loads = [
+        pltpu.make_async_copy(w1_hbm, w1_ref, load_sem.at[0]),
+        pltpu.make_async_copy(w2_hbm, w2_ref, load_sem.at[1]),
+    ]
+    for load in loads:
+        load.start()
     barrier = pltpu.get_barrier_semaphore()
     rec_bits = [s for s in orders[0] if s[0] == "rec"]
     for d in range(1, tm):
@@ -85,7 +91,7 @@
         )
         copy.start()
         edges.append(copy)
-    for copy in edges:
+    for copy in edges[:2]:
         copy.wait()
 
     row = lax.broadcasted_iota(jnp.int32, x_ref.shape, 0)
@@ -159,6 +165,7 @@
     lax.fori_loop(0, rows_all // STEP, first_act, 0)
     act0_ref[:, 4 * C :] = pltpu.roll(act0_ref[:, :C].astype(F32), rows_all - 1, 0).astype(BF16)
 
+    loads[0].wait()
     pre1_ref[:, :C] = dot(act0_ref[:, : 3 * C], w1_ref[...], 1, 0)
     pre1_ref[:, C:] = dot(act0_ref[:, 2 * C :], w1_ref[...], 1, 0)
 
@@ -174,6 +181,7 @@
     lax.fori_loop(0, rows_all // STEP, second_act, 0)
     act1_ref[:, 2 * C :] = pltpu.roll(act1_ref[:, :C].astype(F32), rows_all - 1, 0).astype(BF16)
 
+    loads[1].wait()
     pre2_ref[...] = dot(act1_ref[...], w2_ref[...], 1, 0)
 
     def third_act(i, carry):
@@ -184,6 +192,7 @@
         return carry
 
     lax.fori_loop(0, rows // STEP, third_act, 0)
+    edges[2].wait()
     slope = gelu_parts(pre2_ref[rows:, :])[1]
     edge = jnp.where(me["tm"] == 0, 0.0, edge_ref[...].astype(F32))
     delta2_ref[rows:, :] = (edge * slope).astype(BF16)
@@ -347,7 +356,7 @@
 
     launch_small()
     while min(s["step"] for s in state) <= 2 * stages:
-        for part in range(parts):
+        for part in (3, 4, 5, 0, 1, 2):
             if state[part]["step"] <= 2 * stages:
                 advance(part)
         if len(small_copies) < stages:
@@ -385,7 +394,7 @@
             jax.ShapeDtypeStruct((total_rows, C), BF16),
             jax.ShapeDtypeStruct((16, C), F32),
         ),
-        in_specs=[vmem] * 7,
+        in_specs=[vmem] * 4 + [pl.BlockSpec(memory_space=pltpu.HBM)] * 2 + [vmem],
         out_specs=(vmem,) * 3,
         scratch_shapes=[
             pltpu.VMEM((rows_all, 4 * C), F32),
@@ -411,6 +420,9 @@
             pltpu.VMEM((2, tm, 2, C), F32),
             pltpu.VMEM((stages + 1, 16, C), F32),
             pltpu.VMEM((stages, 16, C), F32),
+            pltpu.VMEM((3 * C, C), BF16),
+            pltpu.VMEM((3 * C, C), BF16),
+            pltpu.SemaphoreType.DMA((2,)),
             pltpu.SemaphoreType.DMA((3,)),
             pltpu.SemaphoreType.DMA((3,)),
             pltpu.SemaphoreType.DMA((6, 2 * stages)),

time: 78 us -> 75.1 us (0.963)
  Pallas kernels: 64.4 us -> 61.5 us
    pallas_call x1, Pallas kernels: 64.4 us -> 61.5 us  [shards(): pl.pallas_call(functools.partial(kernel, tm, rec), out_shape=(jax.ShapeDt...]
where the time goes in v3:
time: 75.1 us; the launch traced here: 74.8 us
  Pallas kernels  61.5 us (82%)
  other arithmetic  6.9 us (9%)
  local copies, waits for them, and re-layouts  5.65 us (8%)
    pallas_call x1, Pallas kernels, shards(): pl.pallas_call(functools.partial(kernel, tm, rec), out_shape=(jax.ShapeDt...  61.5 us
    convert_element_type x1, other arithmetic, shards(): grad_two = res[:3 * C].astype(F32)  5.48 us
    unnamed x9, local copies, waits for them, and re-layouts  4.14 us

profile of v3, /device:TPU:0, one launch (start us, length us, event | category | flops | bytes accessed | tf_op | source)
XLA Modules:
  0.0 74.8 jit_solution(13669889344445556902)
XLA Ops:
  0.6 0.5 broadcast.7
  1.1 1.4 %reduce.3 = f32[5120]{0:T(1024)S(1)} reduce(f32[1,5120]{1,0:T(1,128)} %param.7, f32[]{:T(128)} %broadcast.7), dimensions={0}, to_apply=%param.7.reduce_sub_computation.3 | reduce | bytes 40964 | tf_op args[0]
  2.6 0.8 %concatenate.3.taps_ref = f32[32,512]{1,0:T(8,128)S(1)} pad(f32[10,512]{1,0:T(8,128)} %param.8, f32[]{:T(128)} %constant.1.clone.1), padding=0_22x0_0 | pad | bytes 86020 | tf_op jit(solution)/shard_map/concatenate | solution.py:386
  3.3 0.1 reshape.15
  3.5 0.0 copy-start
  3.5 0.9 %copy-done = bf16[1,256,512]{2,1,0:T(8,128)(2,1)S(1)} copy-done((bf16[1,256,512]{2,1,0:T(8,128)(2,1)S(1)}, bf16[1,256,512]{2,1,0:T(8,128)(2,1)}, u32[]{:S(2)}) %copy-start) | copy-done | bytes 262168
  4.5 0.0 copy-start.1
  4.5 0.7 copy-done.1
  5.1 0.0 copy-start.2
  5.1 0.7 copy-done.2
  5.8 61.5 %shard_map.118 = (bf16[256,512]{1,0:T(8,128)(2,1)S(1)}, bf16[3072,512]{1,0:T(8,128)(2,1)}, f32[16,512]{1,0:T(8,128)S(1)}) custom-call(f32[256,128]{1,0:T(8,128)S(1)} %pad.5.audio_ref, f32[32,512]{1,0:T(8,128)S(1)} %concatenate.3.taps_ref, f32[1,512]{1,0:T(1,128)S(1)} %bitcast.10, f32[1,512]{1,0:T(1,128)S(1)} %bitcast.11, bf16[1536,512]{1,0:T(8,128)(2,1)} %w1_hbm.1, ...), custom_call_target="tpu_custom_call" | custom-call | tf_op jit(solution)/shard_map/pallas_call | solution.py:390
  67.4 0.6 fusion
  68.0 5.5 %slice_convert_fusion = (f32[1536,512]{1,0:T(8,128)}, f32[1536,512]{1,0:T(8,128)}) fusion(bf16[3072,512]{1,0:T(8,128)(2,1)} %get-tuple-element.11), kind=kLoop, calls=%fused_computation | loop fusion | flops 1572864 | bytes 9437184 | tf_op jit(solution)/shard_map/convert_element_type | solution.py:439
  73.4 0.7 copy.15
  74.2 0.6 copy.16
  (1 shorter events, 0.0 us)
Async XLA Ops:
  3.5 1.0 %copy-start = (bf16[1,256,512]{2,1,0:T(8,128)(2,1)S(1)}, bf16[1,256,512]{2,1,0:T(8,128)(2,1)}, u32[]{:S(2)}) copy-start(bf16[1,256,512]{2,1,0:T(8,128)(2,1)} %param.13) | copy-start | bytes 786436
  4.5 0.7 copy-start.1
  5.1 0.7 copy-start.2
